TPU v7x, 32 devices: a whole 2x2x4 slice. The times are simulated.
32 devices in a mesh: frame: 8 (over z, x), head: 4 (over y, core).
Axes of the slice: x: 2, y: 2, z: 4, core: 2. Of those that a mesh axis runs over, the one named last changes fastest.
Arguments:
- query_proj: bfloat16 [16, 12288, 128], P('head', 'frame'), may hold values from -6 to 6
- key_proj: bfloat16 [16, 12288, 128], P('head', 'frame'), may hold values from -6 to 6
- value_proj: bfloat16 [16, 12288, 128], P('head', 'frame'), may hold values from -6 to 6
- lengths: int32 [16], replicated, may hold values from 384 to 1536, as said below
- out_weight: bfloat16 [1024, 1024], P('head'), may hold values from -0.1875 to 0.1875
Outputs:
- projected: bfloat16 [24576, 1024], P(('frame', 'head'))
Inputs may be any that keep to these rules, and one draw needn't show every extreme that they name: `lengths`: some frame has all 1536 tokens valid.
All inputs are finite; a program needn't handle non-finite values.
Results may differ from a plain program's by a relative error of at most 0.0057.
Values may be sent and summed in bfloat16 or wider, within the bound.
No kernel may reach another device: no remote copies, remote signals or barrier semaphores. Data moves between devices by JAX's collectives and lax.ppermute only.
A program may use at most 192 MiB of HBM per device.

v0:
```python
import functools
import math

import jax
import jax.numpy as jnp
from jax import lax
from jax.experimental import pallas as pl
from jax.experimental.pallas import tpu as pltpu
from jax.sharding import PartitionSpec as P

LANES = 128
STRIDES = (0, 1, 4, 16)
VMEM = 20 * 1024 * 1024
LOW = -1e30
WIDTH = 256


def swapped(x):
    return pltpu.roll(x, LANES // 2, 1)


def doubled(blocks):
    mask = (lax.broadcasted_iota(jnp.int32, (16, LANES), 1) < LANES // 2).astype(blocks[0].dtype)[:1]
    even = [block * mask for block in blocks]
    odd = [block - part for block, part in zip(blocks, even)]
    return jnp.concatenate([part + swapped(part) for part in even + odd], axis=0)


def matmul(a, b):
    return jnp.dot(a, b, preferred_element_type=jnp.float32)


def attend_kernel(slots, scale, half, width, has_state, final, meta_ref, q_ref, *refs):
    refs = list(refs)
    key_refs = [refs.pop(0) for _ in slots]
    value_refs = [refs.pop(0) for _ in slots]
    if has_state:
        state_ref, marks_ref = refs.pop(0), refs.pop(0)
    if final:
        if len(refs) > 6:
            refs.pop(0)
        out_ref = refs.pop(0)
    else:
        out_ref, mark_ref = refs.pop(0), refs.pop(0)
    q2_ref, even_ref, odd_ref, acc_ref, top_ref = refs
    if not final:
        acc_ref = out_ref
    pairs = q_ref.shape[0]
    size = LANES // 2
    depth = acc_ref.shape[0]
    tokens = 2 * pairs
    block = 2 * half
    counts = [meta_ref[slot] for slot in slots]
    blocks = [(count + block - 1) // block for count in counts]
    total = sum(blocks)

    scaled = jnp.transpose(q_ref[...]).astype(jnp.float32) * scale
    high = scaled.astype(jnp.bfloat16)
    low = (scaled - high.astype(jnp.float32)).astype(jnp.bfloat16)
    q2_ref[:size, :pairs] = high[:size]
    q2_ref[size:, :pairs] = low[:size]
    q2_ref[:size, pairs:] = high[size:]
    q2_ref[size:, pairs:] = low[size:]
    acc_ref[...] = jnp.zeros(acc_ref.shape, acc_ref.dtype)

    largest = None
    for key_ref in key_refs:
        top = jnp.max(jnp.abs(key_ref[...]), axis=0, keepdims=True).astype(jnp.float32)
        largest = top if largest is None else jnp.maximum(largest, top)
    largest = jnp.broadcast_to(largest, (8, LANES))
    largest = jnp.maximum(largest, swapped(largest))
    key_square = jnp.sum(largest * largest, axis=1, keepdims=True) * 0.5
    square = scaled * scaled
    longest = jnp.maximum(
        jnp.sum(square[:size], axis=0, keepdims=True), jnp.sum(square[size:], axis=0, keepdims=True)
    )
    product = jnp.max(longest, axis=1, keepdims=True) * key_square[:1]
    if has_state:
        product = jnp.where(marks_ref[:1, :1] > 0.0, 1e30, product)
    safe = jnp.max(product) * 1.01 < 1e4

    token = 2 * lax.broadcasted_iota(jnp.int32, (8, pairs), 1)
    for at, (value_ref, count) in enumerate(zip(value_refs, counts)):
        turned = jnp.transpose(value_ref[...])
        cols = slice(at * pairs, (at + 1) * pairs)
        for ref, part, later in ((even_ref, turned[:size], 0), (odd_ref, turned[size:], 1)):
            valid = (token + later < count).astype(jnp.float32)[:1].astype(ref.dtype)
            ref[:size, cols] = part * valid
            ref[size:, cols] = jnp.broadcast_to(valid, (depth - size, pairs))

    def place_of(index):
        which, start, rest = 0, 0, index
        for at, number in enumerate(blocks):
            here = (rest >= 0) & (rest < number)
            which = jnp.where(here, at, which)
            start = jnp.where(here, rest * half, start)
            rest = rest - number
        return which, pl.multiple_of(start, half)

    def keys_of(index):
        which, start = place_of(index)
        rows = pl.ds(start, half)
        keys = key_refs[0][rows, :]
        for at in range(1, len(slots)):
            keys = jnp.where(which == at, key_refs[at][rows, :], keys)
        return keys

    def values_at(first, number):
        cols = []
        for i in range(number):
            which, start = place_of(first + i)
            cols.append(pl.ds(pl.multiple_of(which * pairs + start, half), half))
        return jnp.concatenate([ref[:, at] for ref in (even_ref, odd_ref) for at in cols], axis=1)

    def tiles(parts):
        steps = []
        for first, number in parts:
            keys = doubled([keys_of(first + i) for i in range(number)])
            values = values_at(first, number)
            steps += [(keys, values, at) for at in range(0, tokens, width)]

        def scores_at(step):
            keys, _, at = step
            return matmul(keys, q2_ref[:, at : at + width])

        scores = scores_at(steps[0])
        for step, after in zip(steps, steps[1:] + [None]):
            _, values, at = step
            later = scores_at(after) if after is not None else None
            acc_ref[:, at : at + width] += matmul(values, jnp.exp2(scores).astype(jnp.bfloat16))
            scores = later

    @pl.when(safe)
    def _():
        def whole(index, carry):
            tiles([(index * 4, 2), (index * 4 + 2, 2)])
            return carry

        lax.fori_loop(0, total // 4, whole, 0)

        @pl.when(total % 4 >= 2)
        def _():
            tiles([(total // 4 * 4, 2)])

        @pl.when(total % 2 == 1)
        def _():
            tiles([(total - 1, 1)])

    @pl.when(jnp.logical_not(safe))
    def _():
        if has_state:
            marked = jnp.max(marks_ref[...]) > 0.0
            rows = state_ref[...]
            row = lax.broadcasted_iota(jnp.int32, rows.shape, 0)
            acc_ref[...] = jnp.where(marked & (row >= size), 1.0, rows)
            top_ref[...] = jnp.where(marked, rows[size : size + 8], 0.0)
        else:
            top_ref[...] = jnp.full(top_ref.shape, LOW)
        step = 2 * half
        row = lax.broadcasted_iota(jnp.int32, (block, step), 0)
        token = jnp.where(row < half, 2 * row, 2 * (row - half) + 1)
        for at_source, (key_ref, count, number) in enumerate(zip(key_refs, counts, blocks)):

            def one(index, carry, at_source=at_source, key_ref=key_ref, count=count):
                start = pl.multiple_of(index * half, half)
                keys = doubled([key_ref[pl.ds(start, half), :]])
                cols = pl.ds(pl.multiple_of(at_source * pairs + start, half), half)
                values = jnp.concatenate([even_ref[:, cols], odd_ref[:, cols]], axis=1)

                def part(i, carry):
                    at = pl.ds(pl.multiple_of(i * step, step), step)
                    scores = jnp.where(token < count - index * block, matmul(keys, q2_ref[:, at]), LOW)
                    before = top_ref[:, at]
                    top = jnp.maximum(before, jnp.max(scores, axis=0, keepdims=True))
                    weights = jnp.exp2(scores - top[:1]).astype(jnp.bfloat16)
                    acc_ref[:, at] = acc_ref[:, at] * jnp.exp2(before - top)[:1] + matmul(values, weights)
                    top_ref[:, at] = top
                    return carry

                return lax.fori_loop(0, tokens // step, part, carry)

            lax.fori_loop(0, number, one, 0)

        if not final:
            rows = acc_ref[...]
            sums = rows[size : size + 1]
            row = lax.broadcasted_iota(jnp.int32, rows.shape, 0)
            acc_ref[...] = jnp.where(row < size, rows / sums, top_ref[:1, :] + jnp.log2(sums))

    if not final:
        mark_ref[...] = jnp.broadcast_to(jnp.where(safe, 0.0, 1.0), mark_ref.shape)
        return
    rows = acc_ref[...]
    if has_state:
        rows = rows + state_ref[...] * jnp.where(safe, 1.0, 0.0)
    result = (rows[:size] * (1.0 / rows[size : size + 1])).astype(out_ref.dtype)
    result = jnp.transpose(jnp.concatenate([result[:, :pairs], result[:, pairs:]], axis=0))
    out_ref[...] = result.reshape(out_ref.shape)


def attend(meta, queries, within, first_head, heads, sources, state, dests, out, name):
    pairs = queries.shape[1] // 2
    head_size = LANES // 2
    scale = math.log2(math.e) / math.sqrt(head_size)
    half = min(128, pairs)
    width = min(WIDTH, 2 * pairs)
    depth = head_size + 16

    def spec(lead, part, start):
        if lead is None:
            return pl.BlockSpec((None, pairs, LANES), lambda h, m: (h + start, part, 0))
        return pl.BlockSpec((None, None, pairs, LANES), lambda h, m: (lead, h + start, part, 0))

    in_specs, arrays = [spec(None, within, first_head)], [queries]
    for part in (1, 2):
        for source in sources:
            array, lead, part_of, start = source[part]
            in_specs.append(spec(lead, part_of, start))
            arrays.append(array)
    shapes = [(depth, 2 * pairs), (8, LANES)]
    if state is not None:
        sums, marks, start = state
        in_specs += [pl.BlockSpec((None, *shape), lambda h, m: (h + start, 0, 0)) for shape in shapes]
        arrays += [sums, marks]
    aliases = {}
    if dests is None:
        out_shape = [jax.ShapeDtypeStruct((heads, *shape), jnp.float32) for shape in shapes]
        out_spec = [pl.BlockSpec((None, *shape), lambda h, m: (h, 0, 0)) for shape in shapes]
    else:
        out_shape = jax.ShapeDtypeStruct((2 * dests, heads, pairs // dests, LANES), jnp.bfloat16)
        out_spec = pl.BlockSpec((dests, 1, pairs // dests, LANES), lambda h, m: (within, h, 0, 0))
        if out is not None:
            in_specs.append(pl.BlockSpec(memory_space=pl.ANY))
            aliases = {1 + len(arrays): 0}
            arrays.append(out)
    unpacked = len(sources) * pairs
    work = heads * len(sources) * (2 * pairs) ** 2
    return pl.pallas_call(
        functools.partial(
            attend_kernel,
            tuple(source[0] for source in sources),
            scale,
            half,
            width,
            state is not None,
            dests is not None,
        ),
        out_shape=out_shape,
        grid_spec=pltpu.PrefetchScalarGridSpec(
            num_scalar_prefetch=1,
            grid=(heads,),
            in_specs=in_specs,
            out_specs=out_spec,
            scratch_shapes=[
                pltpu.VMEM((LANES, 2 * pairs), jnp.bfloat16),
                pltpu.VMEM((depth, unpacked), jnp.bfloat16),
                pltpu.VMEM((depth, unpacked), jnp.bfloat16),
                pltpu.VMEM((depth, 2 * pairs), jnp.float32),
                pltpu.VMEM((8, 2 * pairs), jnp.float32),
            ],
        ),
        input_output_aliases=aliases,
        compiler_params=pltpu.CompilerParams(vmem_limit_bytes=VMEM),
        cost_estimate=pl.CostEstimate(
            flops=work * head_size * (16 if dests is None else 4), bytes_accessed=8 * heads * pairs * LANES * 2, transcendentals=work
        ),
        name=name,
    )(meta, *arrays)


def project_kernel(layout, rows, size, weight_ref, part_ref, *refs):
    out_ref = refs[-1]
    lane = lax.broadcasted_iota(jnp.int32, (rows, LANES), 1) < LANES // 2
    even, odd, weights = [], [], []
    for first in range(0, len(layout), 2):
        (s, k, head), (s2, k2, head2) = layout[first], layout[first + 1]
        a = part_ref[s, k].astype(jnp.float32)
        b = part_ref[s2, k2].astype(jnp.float32)
        even.append(jnp.where(lane, a, swapped(b)).astype(jnp.bfloat16))
        odd.append(jnp.where(lane, swapped(a), b).astype(jnp.bfloat16))
        weights += [weight_ref[h * size : (h + 1) * size, :] for h in (head, head2)]
    stacked = jnp.concatenate([jnp.concatenate(even, axis=1), jnp.concatenate(odd, axis=1)], axis=0)
    token = lax.broadcasted_iota(jnp.int32, (2 * rows, 2 * rows), 0)
    place = lax.broadcasted_iota(jnp.int32, (2 * rows, 2 * rows), 1)
    order = (place == token // 2 + (token % 2) * rows).astype(jnp.bfloat16)
    tokens = matmul(order, stacked).astype(jnp.bfloat16)
    result = matmul(tokens, jnp.concatenate(weights, axis=0))
    if len(refs) > 1:
        result = result + refs[0][...]
    out_ref[...] = result.astype(out_ref.dtype)


def project(part, layout, weight, before, last):
    pairs = part.shape[2]
    rows = LANES if pairs % LANES == 0 else pairs
    out = pl.BlockSpec((2 * rows, weight.shape[1]), lambda i: (i, 0))
    return pl.pallas_call(
        functools.partial(project_kernel, layout, rows, LANES // 2),
        out_shape=jax.ShapeDtypeStruct((2 * pairs, weight.shape[1]), jnp.bfloat16 if last else jnp.float32),
        grid=(pairs // rows,),
        in_specs=[
            pl.BlockSpec(weight.shape, lambda i: (0, 0)),
            pl.BlockSpec((*part.shape[:2], rows, LANES), lambda i: (0, 0, i, 0)),
        ]
        + [out] * (before is not None),
        out_specs=out,
        compiler_params=pltpu.CompilerParams(vmem_limit_bytes=20 * 1024 * 1024),
        cost_estimate=pl.CostEstimate(
            flops=4 * pairs * LANES // 2 * len(layout) * weight.shape[1], bytes_accessed=8 * 2**20, transcendentals=0
        ),
        name="project",
    )(weight, part, *([] if before is None else [before]))


def shifted(x, pairs):
    return lax.ppermute(x, "frame", pairs)


def shards(query_proj, key_proj, value_proj, lengths, out_weight):
    devices = lax.axis_size("frame")
    groups = lax.axis_size("head")
    index = lax.axis_index("frame")
    heads, rows, _ = query_proj.shape
    half = rows // 2
    frames = lengths.shape[0]
    weight = lax.all_gather(out_weight, "head", axis=0, tiled=True)

    wanted = jnp.stack([2 * index + within - stride for within in range(2) for stride in STRIDES])
    table = jnp.arange(frames, dtype=jnp.int32)
    meta = jnp.sum(jnp.where(wanted[:, None] == table[None, :], lengths[None, :], 0), axis=1, dtype=jnp.int32)
    meta = jnp.minimum(meta, rows)

    size = heads // 2 if heads % 2 == 0 else heads
    starts = range(0, heads, size)
    by_two = [(i, i + 2) for i in range(devices - 2)]
    first = jnp.stack((key_proj[:, :half], value_proj[:, :half]))
    lasts = [
        jnp.stack((key_proj[start : start + size, half:], value_proj[start : start + size, half:]))
        for start in starts
    ]
    near_lasts = [shifted(last, by_two) for last in lasts]
    far = None
    if devices > 8:
        both = jnp.stack((key_proj, value_proj))
        far = shifted(both, [(i, i + 8) for i in range(devices - 8)])

    def own(slot, part, start):
        return slot, (key_proj, None, part, start), (value_proj, None, part, start)

    def moved(slot, array, part, start):
        return slot, (array, 0, part, start), (array, 1, part, start)

    state_last = {}
    for start in starts[:-1]:
        sources = [own(4, 1, start), own(5, 0, start)]
        sums, marks = attend(meta, query_proj, 1, start, size, sources, None, None, None, "last_own")
        state_last[start] = (sums, marks, 0)
        first, near_lasts[0], sums = lax.optimization_barrier((first, near_lasts[0], sums))
        state_last[start] = (sums, marks, 0)
    near_first = shifted(first, by_two)
    near_lasts[0], held = lax.optimization_barrier((near_lasts[0], query_proj))
    sums_first, marks_first = attend(meta, held, 0, 0, heads, [own(0, 0, 0)], None, None, None, "first_own")
    if len(starts) > 1:
        near_lasts[1], sums_first = lax.optimization_barrier((near_lasts[1], sums_first))
    to_even = [(i + 1, i) for i in range(2, devices - 1, 2)]
    to_odd = [(i, i + 1) for i in range(0, devices - 1, 2)]
    prevs = [
        shifted(jnp.where(index % 2 == 0, last, near), to_even + to_odd) for last, near in zip(lasts, near_lasts)
    ]
    dests = groups // 2
    outs = []
    for number, start in enumerate(starts):
        sources = [moved(6, near_lasts[number], 0, 0)]
        if far is not None:
            sources.append(moved(7, far, 1, start))
        state = state_last.get(start)
        if state is None:
            sources += [own(4, 1, start), own(5, 0, start)]
        outs.append(attend(meta, query_proj, 1, start, size, sources, state, dests, None, "last_rest"))
    weight, *outs = lax.optimization_barrier((weight, *outs))
    result = None
    for number, start in enumerate(starts):
        sources = [moved(1, prevs[number], 0, 0), moved(2, near_first, 0, start)]
        if far is not None:
            sources.append(moved(3, far, 0, start))
        state = (sums_first, marks_first, start)
        out = attend(meta, query_proj, 0, start, size, sources, state, dests, outs[number], "first_rest")
        got = lax.all_to_all(out, "head", split_axis=0, concat_axis=0, tiled=True)
        layout = tuple(
            (head // heads, head % heads - start, head)
            for head in range(groups * heads)
            if start <= head % heads < start + size
        )
        result = project(got, layout, weight, result, start == starts[-1])
    return result


def solution(mesh):
    return jax.shard_map(
        shards,
        mesh=mesh,
        in_specs=(
            P("head", "frame", None),
            P("head", "frame", None),
            P("head", "frame", None),
            P(),
            P("head", None),
        ),
        out_specs=P(("frame", "head"), None),
        check_vma=False,
    )
```

profile of v0, /device:TPU:16, one launch (start us, length us, event | category | flops | bytes accessed | tf_op | source)
XLA Modules:
  0.0 414.6 jit_solution(7901894152950879092)
XLA Ops:
  6.5 0.7 all-gather.2.cloned.1.call-update
  7.3 1.5 slice_bitcast_fusion.2
  8.8 1.0 pad_maximum_fusion.1
  9.7 3.6 collective-permute-start
  13.4 1.0 pad_maximum_fusion.2
  14.4 1.9 collective-permute-start.1
  16.3 0.1 slice_bitcast_fusion
  16.4 1.3 pad_maximum_fusion
  17.8 0.2 select_reduce_fusion
  18.0 1.5 copy-done.6
  19.5 58.0 %last_own.1 = (f32[2,80,1536]{2,1,0:T(8,128)S(1)}, f32[2,8,128]{2,1,0:T(8,128)S(1)}) custom-call(s32[8]{0:T(128)S(1)} %broadcast_minimum_fusion.meta_ref, bf16[4,1536,128]{2,1,0:T(8,128)(2,1)S(1)} %copy-done.6, bf16[4,1536,128]{2,1,0:T(8,128)(2,1)S(1)} %copy-done.5, bf16[4,1536,128]{2,1,0:T(8,128)(2,1)S(1)} %copy-done.5, ...), custom_call_target="tpu_custom_call" | custom-call | flops 9663676416 | bytes 3145728 | tf_op jit(solution)/shard_map/last_own/pallas_call | solution.py:238
  77.5 1.0 broadcast_select_fusion
  78.6 2.0 collective-permute-start.4
  80.6 1.9 collective-permute-start.3
  82.6 53.5 %first_own.1 = (f32[4,80,1536]{2,1,0:T(8,128)S(1)}, f32[4,8,128]{2,1,0:T(8,128)S(1)}) custom-call(s32[8]{0:T(128)S(1)} %broadcast_minimum_fusion.meta_ref, bf16[4,1536,128]{2,1,0:T(8,128)(2,1)S(1)} %copy-done.6, bf16[4,1536,128]{2,1,0:T(8,128)(2,1)S(1)} %copy-done.5, bf16[4,1536,128]{2,1,0:T(8,128)(2,1)S(1)} %copy-done.4), custom_call_target="tpu_custom_call" | custom-call | flops 9663676416 | bytes 6291456 | tf_op jit(solution)/shard_map/first_own/pallas_call | solution.py:238
  136.1 1.1 broadcast_select_fusion.1
  137.2 5.7 %collective-permute-start.2 = (bf16[2,2,768,128]{3,2,1,0:T(8,128)(2,1)}, bf16[2,2,768,128]{3,2,1,0:T(8,128)(2,1)}, u32[]{:S(2)}, u32[]{:S(2)}) collective-permute-start(bf16[2,2,768,128]{3,2,1,0:T(8,128)(2,1)} %broadcast_select_fusion.1), channel_id=1, source_target_pairs={{12,8},{20,16},{28,24},{0,4},{8,12},{16,20},{24,28},{13,9},{21,17}... | collective-permute-start | bytes 2359304 | tf_op jit(solution)/shard_map/ppermute | solution.py:316
  142.9 80.6 %last_rest.3.refs_6_ = bf16[4,2,384,128]{3,2,1,0:T(8,128)(2,1)} custom-call(s32[8]{0:T(128)S(1)} %broadcast_minimum_fusion.meta_ref, bf16[4,1536,128]{2,1,0:T(8,128)(2,1)S(1)} %copy-done.6, bf16[2,2,768,128]{3,2,1,0:T(8,128)(2,1)} %collective-permute-done.1.refs_0_.refs_3_, bf16[4,1536,128]{2,1,0:T(8,128)(2,1)S(1)} %copy-done.5, ...), custom_call_target="tpu_custom_call" | custom-call | flops 3623878656 | bytes 3145728 | tf_op jit(solution)/shard_map/last_rest/pallas_call | solution.py:238
  223.5 24.0 %last_rest.2.refs_6_ = bf16[4,2,384,128]{3,2,1,0:T(8,128)(2,1)} custom-call(s32[8]{0:T(128)S(1)} %broadcast_minimum_fusion.meta_ref, bf16[4,1536,128]{2,1,0:T(8,128)(2,1)S(1)} %copy-done.6, bf16[2,2,768,128]{3,2,1,0:T(8,128)(2,1)} %collective-permute-done.refs_0_.refs_1_, bf16[2,2,768,128]{3,2,1,0:T(8,128)(2,1)} %collective-permute-done.refs_0_.refs_1_, ...), custom_call_target="tpu_custom_call" | custom-call | flops 1207959552 | bytes 3145728 | tf_op jit(solution)/shard_map/last_rest/pallas_call | solution.py:238
  247.5 1.5 copy-done.9
  249.1 65.4 %first_rest.3 = bf16[4,2,384,128]{3,2,1,0:T(8,128)(2,1)} custom-call(s32[8]{0:T(128)S(1)} %broadcast_minimum_fusion.meta_ref, bf16[4,1536,128]{2,1,0:T(8,128)(2,1)S(1)} %copy-done.7, bf16[2,2,768,128]{3,2,1,0:T(8,128)(2,1)} %collective-permute-done.4.refs_0_.refs_2_, ...), custom_call_target="tpu_custom_call", output_to_operand_aliasing={{}: (8, {})} | custom-call | flops 2415919104 | bytes 3145728 | tf_op jit(solution)/shard_map/first_rest/pallas_call | solution.py:238
  314.5 3.7 all-to-all-start.1
  318.2 1.5 copy-done.10
  319.8 65.4 %first_rest.2 = bf16[4,2,384,128]{3,2,1,0:T(8,128)(2,1)} custom-call(s32[8]{0:T(128)S(1)} %broadcast_minimum_fusion.meta_ref, bf16[4,1536,128]{2,1,0:T(8,128)(2,1)S(1)} %copy-done.7, bf16[2,2,768,128]{3,2,1,0:T(8,128)(2,1)} %collective-permute-done.2.refs_0_.refs_2_, ...), custom_call_target="tpu_custom_call", output_to_operand_aliasing={{}: (8, {})} | custom-call | flops 2415919104 | bytes 3145728 | tf_op jit(solution)/shard_map/first_rest/pallas_call | solution.py:238
  385.2 0.9 copy-done.2
  386.1 4.2 %all-to-all-start = ((bf16[4,2,384,128]{3,2,1,0:T(8,128)(2,1)}), bf16[4,2,384,128]{3,2,1,0:T(8,128)(2,1)}, u32[]{:S(2)}, u32[]{:S(2)}) async-start(bf16[4,2,384,128]{3,2,1,0:T(8,128)(2,1)} %first_rest.2), calls=%async_computation | async-start | bytes 1572864 | tf_op jit(solution)/shard_map/all_to_all | solution.py:388
  390.3 1.6 copy-done
  391.9 1.1 copy-done.3
  393.0 2.0 project.2.refs_0_
  395.0 7.0 %all-to-all-done.part_ref = bf16[4,2,384,128]{3,2,1,0:T(8,128)(2,1)} async-done(((bf16[4,2,384,128]{3,2,1,0:T(8,128)(2,1)}), bf16[4,2,384,128]{3,2,1,0:T(8,128)(2,1)}, u32[]{:S(2)}, u32[]{:S(2)}) %all-to-all-start) | async-done | bytes 786464 | tf_op jit(solution)/shard_map/all_to_all | solution.py:388
  402.0 1.6 copy-done.1
  403.6 4.2 %project.3 = bf16[768,1024]{1,0:T(8,128)(2,1)} custom-call(bf16[1024,1024]{1,0:T(8,128)(2,1)S(1)} %copy-done.1, bf16[4,2,384,128]{3,2,1,0:T(8,128)(2,1)} %all-to-all-done.part_ref, f32[768,1024]{1,0:T(8,128)S(1)} %project.2.refs_0_), custom_call_target="tpu_custom_call" | custom-call | flops 805306368 | bytes 8388608 | tf_op jit(solution)/shard_map/project/pallas_call | solution.py:297
  (39 shorter events, 0.2 us)
Async XLA Ops:
  6.5 241.0 %all-gather.2.cloned.1.call-start = ((), (), s32[]{:S(2)}) async-start(), calls=%async_computation.2 | async-start | bytes 2621440 | tf_op jit(solution)/shard_map/all_gather | solution.py:326
  8.7 5.6 %copy-start.11 = (bf16[1,2,768,128]{3,2,1,0:T(8,128)(2,1)}, bf16[1,2,768,128]{3,2,1,0:T(8,128)(2,1)S(1)}, u32[]{:S(2)}) copy-start(bf16[1,2,768,128]{3,2,1,0:T(8,128)(2,1)S(1)} %get-tuple-element.35) | copy-start | bytes 1179652
  8.7 5.6 %copy-start.13 = (bf16[1,2,768,128]{3,2,1,0:T(8,128)(2,1)}, bf16[1,2,768,128]{3,2,1,0:T(8,128)(2,1)S(1)}, u32[]{:S(2)}) copy-start(bf16[1,2,768,128]{3,2,1,0:T(8,128)(2,1)S(1)} %get-tuple-element.40) | copy-start | bytes 1179652
  8.7 5.6 %copy-start.15 = (bf16[1,2,768,128]{3,2,1,0:T(8,128)(2,1)}, bf16[1,2,768,128]{3,2,1,0:T(8,128)(2,1)S(1)}, u32[]{:S(2)}) copy-start(bf16[1,2,768,128]{3,2,1,0:T(8,128)(2,1)S(1)} %get-tuple-element.39) | copy-start | bytes 1179652
  8.8 7.5 %copy-start.4 = (bf16[4,1536,128]{2,1,0:T(8,128)(2,1)S(1)}, bf16[4,1536,128]{2,1,0:T(8,128)(2,1)}, u32[]{:S(2)}) copy-start(bf16[4,1536,128]{2,1,0:T(8,128)(2,1)} %refs_5_.1) | copy-start | bytes 4718596
  8.8 7.5 %copy-start.5 = (bf16[4,1536,128]{2,1,0:T(8,128)(2,1)S(1)}, bf16[4,1536,128]{2,1,0:T(8,128)(2,1)}, u32[]{:S(2)}) copy-start(bf16[4,1536,128]{2,1,0:T(8,128)(2,1)} %refs_2_.3) | copy-start | bytes 4718596
  9.7 67.8 %collective-permute-start = (bf16[2,2,768,128]{3,2,1,0:T(8,128)(2,1)}, bf16[2,2,768,128]{3,2,1,0:T(8,128)(2,1)}, u32[]{:S(2)}, u32[]{:S(2)}) collective-permute-start(bf16[2,2,768,128]{3,2,1,0:T(8,128)(2,1)} %pad_maximum_fusion.1), channel_id=1, source_target_pairs={{0,8},{4,12},{8,16},{12,20},{16,24},{20,28},{1,9},{5,13},{9,17},{1... | collective-permute-start | bytes 2359304 | tf_op jit(solution)/shard_map/ppermute | solution.py:316
  14.4 121.7 %collective-permute-start.1 = (bf16[2,2,768,128]{3,2,1,0:T(8,128)(2,1)}, bf16[2,2,768,128]{3,2,1,0:T(8,128)(2,1)}, u32[]{:S(2)}, u32[]{:S(2)}) collective-permute-start(bf16[2,2,768,128]{3,2,1,0:T(8,128)(2,1)} %pad_maximum_fusion.2), channel_id=1, source_target_pairs={{0,8},{4,12},{8,16},{12,20},{16,24},{20,28},{1,9},{5,13},{9,17},{1... | collective-permute-start | bytes 2359304 | tf_op jit(solution)/shard_map/ppermute | solution.py:316
  16.4 1.4 copy-start.17
  18.0 1.5 copy-start.6
  19.5 58.1 %copy-start.16 = (bf16[1,2,768,128]{3,2,1,0:T(8,128)(2,1)S(1)}, bf16[1,2,768,128]{3,2,1,0:T(8,128)(2,1)}, u32[]{:S(2)}) copy-start(bf16[1,2,768,128]{3,2,1,0:T(8,128)(2,1)} %copy-done.15) | copy-start | bytes 1179652
  78.6 57.5 %copy-start.12 = (bf16[1,2,768,128]{3,2,1,0:T(8,128)(2,1)S(1)}, bf16[1,2,768,128]{3,2,1,0:T(8,128)(2,1)}, u32[]{:S(2)}) copy-start(bf16[1,2,768,128]{3,2,1,0:T(8,128)(2,1)} %copy-done.11) | copy-start | bytes 1179652
  78.6 57.5 %copy-start.14 = (bf16[1,2,768,128]{3,2,1,0:T(8,128)(2,1)S(1)}, bf16[1,2,768,128]{3,2,1,0:T(8,128)(2,1)}, u32[]{:S(2)}) copy-start(bf16[1,2,768,128]{3,2,1,0:T(8,128)(2,1)} %copy-done.13) | copy-start | bytes 1179652
  78.6 168.9 %collective-permute-start.4 = (bf16[2,2,768,128]{3,2,1,0:T(8,128)(2,1)}, bf16[2,2,768,128]{3,2,1,0:T(8,128)(2,1)}, u32[]{:S(2)}, u32[]{:S(2)}) collective-permute-start(bf16[2,2,768,128]{3,2,1,0:T(8,128)(2,1)} %broadcast_select_fusion), channel_id=1, source_target_pairs={{12,8},{20,16},{28,24},{0,4},{8,12},{16,20},{24,28},{13,9},{21,17}... | collective-permute-start | bytes 2359304 | tf_op jit(solution)/shard_map/ppermute | solution.py:316
  80.6 166.9 %collective-permute-start.3 = (bf16[2,4,768,128]{3,2,1,0:T(8,128)(2,1)}, bf16[2,4,768,128]{3,2,1,0:T(8,128)(2,1)}, u32[]{:S(2)}, u32[]{:S(2)}) collective-permute-start(bf16[2,4,768,128]{3,2,1,0:T(8,128)(2,1)} %pad_maximum_fusion), channel_id=1, source_target_pairs={{0,8},{4,12},{8,16},{12,20},{16,24},{20,28},{1,9},{5,13},{9,17},{1... | collective-permute-start | bytes 4718600 | tf_op jit(solution)/shard_map/ppermute | solution.py:316
  136.0 87.4 %copy-start.8 = (f32[4,80,1536]{2,1,0:T(8,128)}, f32[4,80,1536]{2,1,0:T(8,128)S(1)}, u32[]{:S(2)}) copy-start(f32[4,80,1536]{2,1,0:T(8,128)S(1)} %get-tuple-element.29.refs_4_) | copy-start | bytes 5898244
  137.2 181.0 %collective-permute-start.2 = (bf16[2,2,768,128]{3,2,1,0:T(8,128)(2,1)}, bf16[2,2,768,128]{3,2,1,0:T(8,128)(2,1)}, u32[]{:S(2)}, u32[]{:S(2)}) collective-permute-start(bf16[2,2,768,128]{3,2,1,0:T(8,128)(2,1)} %broadcast_select_fusion.1), channel_id=1, source_target_pairs={{12,8},{20,16},{28,24},{0,4},{8,12},{16,20},{24,28},{13,9},{21,17}... | collective-permute-start | bytes 2359304 | tf_op jit(solution)/shard_map/ppermute | solution.py:316
  223.5 24.0 %copy-start.7 = (bf16[4,1536,128]{2,1,0:T(8,128)(2,1)S(1)}, bf16[4,1536,128]{2,1,0:T(8,128)(2,1)}, u32[]{:S(2)}) copy-start(bf16[4,1536,128]{2,1,0:T(8,128)(2,1)} %q_ref.10) | copy-start | bytes 4718596
  247.5 1.5 copy-start.9
  314.5 70.7 %all-to-all-start.1 = ((bf16[4,2,384,128]{3,2,1,0:T(8,128)(2,1)}), bf16[4,2,384,128]{3,2,1,0:T(8,128)(2,1)S(1)}, u32[]{:S(2)}, u32[]{:S(2)}) async-start(bf16[4,2,384,128]{3,2,1,0:T(8,128)(2,1)} %first_rest.3), calls=%async_computation.1 | async-start | bytes 1572864 | tf_op jit(solution)/shard_map/all_to_all | solution.py:388
  318.2 1.5 copy-start.10
  385.2 0.9 copy-start.2
  386.1 15.9 %all-to-all-start = ((bf16[4,2,384,128]{3,2,1,0:T(8,128)(2,1)}), bf16[4,2,384,128]{3,2,1,0:T(8,128)(2,1)}, u32[]{:S(2)}, u32[]{:S(2)}) async-start(bf16[4,2,384,128]{3,2,1,0:T(8,128)(2,1)} %first_rest.2), calls=%async_computation | async-start | bytes 1572864 | tf_op jit(solution)/shard_map/all_to_all | solution.py:388
  390.3 1.6 copy-start
  391.9 1.1 copy-start.3
  402.0 1.6 copy-start.1
Sparse Core Ops, SparseCore 0:
  8.9 23.6 all-gather.1
where the time goes:
time: 418 us; the launch traced here: 415 us
  Pallas kernels  353 us (84%)
  starting transfers between devices  23.1 us (6%)
  between operations  13.7 us (3%)
  local copies, waits for them, and re-layouts  11.5 us (3%)
  waiting for transfers between devices  7.71 us (2%)
  other arithmetic  5.58 us (1%)
    pallas_call x6, Pallas kernels, attend(): pl.pallas_call(functools.partial(attend_kernel, tuple((source[0] for sour...  347 us
    ppermute x5, starting transfers between devices, shifted(): return lax.ppermute(x, 'frame', pairs)  15.2 us
    unnamed x36, local copies, waits for them, and re-layouts  9.81 us
  transfers between devices with their start and end apart: 8, of which 1 were waited for; matrix products, arithmetic and copies ran while one was open for 2% of the time, Pallas kernels for 84%

commit v1 on v0

--- a/solution.py
+++ b/solution.py
@@ -11,6 +11,7 @@
 LANES = 128
 STRIDES = (0, 1, 4, 16)
 VMEM = 20 * 1024 * 1024
+WHOLE = 63 * 1024 * 1024
 LOW = -1e30
 WIDTH = 256
 
@@ -19,11 +20,8 @@
     return pltpu.roll(x, LANES // 2, 1)
 
 
-def doubled(blocks):
-    mask = (lax.broadcasted_iota(jnp.int32, (16, LANES), 1) < LANES // 2).astype(blocks[0].dtype)[:1]
-    even = [block * mask for block in blocks]
-    odd = [block - part for block, part in zip(blocks, even)]
-    return jnp.concatenate([part + swapped(part) for part in even + odd], axis=0)
+def unpacked(blocks):
+    return jnp.concatenate(blocks + [swapped(block) for block in blocks], axis=0)[:, : LANES // 2]
 
 
 def matmul(a, b):
@@ -54,13 +52,9 @@
     blocks = [(count + block - 1) // block for count in counts]
     total = sum(blocks)
 
-    scaled = jnp.transpose(q_ref[...]).astype(jnp.float32) * scale
-    high = scaled.astype(jnp.bfloat16)
-    low = (scaled - high.astype(jnp.float32)).astype(jnp.bfloat16)
-    q2_ref[:size, :pairs] = high[:size]
-    q2_ref[size:, :pairs] = low[:size]
-    q2_ref[:size, pairs:] = high[size:]
-    q2_ref[size:, pairs:] = low[size:]
+    turned = jnp.transpose(q_ref[...])
+    q2_ref[:, :pairs] = turned[:size]
+    q2_ref[:, pairs:] = turned[size:]
     acc_ref[...] = jnp.zeros(acc_ref.shape, acc_ref.dtype)
 
     largest = None
@@ -70,14 +64,15 @@
     largest = jnp.broadcast_to(largest, (8, LANES))
     largest = jnp.maximum(largest, swapped(largest))
     key_square = jnp.sum(largest * largest, axis=1, keepdims=True) * 0.5
-    square = scaled * scaled
+    square = turned.astype(jnp.float32)
+    square = square * square
     longest = jnp.maximum(
         jnp.sum(square[:size], axis=0, keepdims=True), jnp.sum(square[size:], axis=0, keepdims=True)
     )
     product = jnp.max(longest, axis=1, keepdims=True) * key_square[:1]
     if has_state:
         product = jnp.where(marks_ref[:1, :1] > 0.0, 1e30, product)
-    safe = jnp.max(product) * 1.01 < 1e4
+    safe = jnp.max(product) * (1.01 * scale * scale) < 1e4
 
     token = 2 * lax.broadcasted_iota(jnp.int32, (8, pairs), 1)
     for at, (value_ref, count) in enumerate(zip(value_refs, counts)):
@@ -115,7 +110,7 @@
     def tiles(parts):
         steps = []
         for first, number in parts:
-            keys = doubled([keys_of(first + i) for i in range(number)])
+            keys = unpacked([keys_of(first + i) for i in range(number)])
             values = values_at(first, number)
             steps += [(keys, values, at) for at in range(0, tokens, width)]
 
@@ -127,7 +122,7 @@
         for step, after in zip(steps, steps[1:] + [None]):
             _, values, at = step
             later = scores_at(after) if after is not None else None
-            acc_ref[:, at : at + width] += matmul(values, jnp.exp2(scores).astype(jnp.bfloat16))
+            acc_ref[:, at : at + width] += matmul(values, jnp.exp2(scores * scale).astype(jnp.bfloat16))
             scores = later
 
     @pl.when(safe)
@@ -163,13 +158,13 @@
 
             def one(index, carry, at_source=at_source, key_ref=key_ref, count=count):
                 start = pl.multiple_of(index * half, half)
-                keys = doubled([key_ref[pl.ds(start, half), :]])
+                keys = unpacked([key_ref[pl.ds(start, half), :]])
                 cols = pl.ds(pl.multiple_of(at_source * pairs + start, half), half)
                 values = jnp.concatenate([even_ref[:, cols], odd_ref[:, cols]], axis=1)
 
                 def part(i, carry):
                     at = pl.ds(pl.multiple_of(i * step, step), step)
-                    scores = jnp.where(token < count - index * block, matmul(keys, q2_ref[:, at]), LOW)
+                    scores = jnp.where(token < count - index * block, matmul(keys, q2_ref[:, at]) * scale, LOW)
                     before = top_ref[:, at]
                     top = jnp.maximum(before, jnp.max(scores, axis=0, keepdims=True))
                     weights = jnp.exp2(scores - top[:1]).astype(jnp.bfloat16)
@@ -252,7 +247,7 @@
             in_specs=in_specs,
             out_specs=out_spec,
             scratch_shapes=[
-                pltpu.VMEM((LANES, 2 * pairs), jnp.bfloat16),
+                pltpu.VMEM((head_size, 2 * pairs), jnp.bfloat16),
                 pltpu.VMEM((depth, unpacked), jnp.bfloat16),
                 pltpu.VMEM((depth, unpacked), jnp.bfloat16),
                 pltpu.VMEM((depth, 2 * pairs), jnp.float32),
@@ -268,45 +263,44 @@
     )(meta, *arrays)
 
 
-def project_kernel(layout, rows, size, weight_ref, part_ref, *refs):
+def project_kernel(rows, weight_ref, part_ref, *refs):
     out_ref = refs[-1]
     lane = lax.broadcasted_iota(jnp.int32, (rows, LANES), 1) < LANES // 2
-    even, odd, weights = [], [], []
-    for first in range(0, len(layout), 2):
-        (s, k, head), (s2, k2, head2) = layout[first], layout[first + 1]
-        a = part_ref[s, k].astype(jnp.float32)
-        b = part_ref[s2, k2].astype(jnp.float32)
+    heads = [part_ref[s, k].astype(jnp.float32) for s in range(part_ref.shape[0]) for k in range(part_ref.shape[1])]
+    even, odd = [], []
+    for a, b in zip(heads[::2], heads[1::2]):
         even.append(jnp.where(lane, a, swapped(b)).astype(jnp.bfloat16))
         odd.append(jnp.where(lane, swapped(a), b).astype(jnp.bfloat16))
-        weights += [weight_ref[h * size : (h + 1) * size, :] for h in (head, head2)]
     stacked = jnp.concatenate([jnp.concatenate(even, axis=1), jnp.concatenate(odd, axis=1)], axis=0)
     token = lax.broadcasted_iota(jnp.int32, (2 * rows, 2 * rows), 0)
     place = lax.broadcasted_iota(jnp.int32, (2 * rows, 2 * rows), 1)
     order = (place == token // 2 + (token % 2) * rows).astype(jnp.bfloat16)
     tokens = matmul(order, stacked).astype(jnp.bfloat16)
-    result = matmul(tokens, jnp.concatenate(weights, axis=0))
+    weight = weight_ref[...]
+    result = matmul(tokens, weight.reshape(-1, weight.shape[-1]))
     if len(refs) > 1:
-        result = result + refs[0][...]
+        result = result + refs[0][...].astype(jnp.float32)
     out_ref[...] = result.astype(out_ref.dtype)
 
 
-def project(part, layout, weight, before, last):
+def project(part, group, weight, before):
     pairs = part.shape[2]
     rows = LANES if pairs % LANES == 0 else pairs
-    out = pl.BlockSpec((2 * rows, weight.shape[1]), lambda i: (i, 0))
+    columns = weight.shape[3]
+    out = pl.BlockSpec((2 * rows, columns), lambda i: (i, 0))
     return pl.pallas_call(
-        functools.partial(project_kernel, layout, rows, LANES // 2),
-        out_shape=jax.ShapeDtypeStruct((2 * pairs, weight.shape[1]), jnp.bfloat16 if last else jnp.float32),
+        functools.partial(project_kernel, rows),
+        out_shape=jax.ShapeDtypeStruct((2 * pairs, columns), jnp.bfloat16),
         grid=(pairs // rows,),
         in_specs=[
-            pl.BlockSpec(weight.shape, lambda i: (0, 0)),
+            pl.BlockSpec((weight.shape[0], None, *weight.shape[2:]), lambda i: (0, group, 0, 0)),
             pl.BlockSpec((*part.shape[:2], rows, LANES), lambda i: (0, 0, i, 0)),
         ]
         + [out] * (before is not None),
         out_specs=out,
-        compiler_params=pltpu.CompilerParams(vmem_limit_bytes=20 * 1024 * 1024),
+        compiler_params=pltpu.CompilerParams(vmem_limit_bytes=WHOLE),
         cost_estimate=pl.CostEstimate(
-            flops=4 * pairs * LANES // 2 * len(layout) * weight.shape[1], bytes_accessed=8 * 2**20, transcendentals=0
+            flops=4 * pairs * weight.size // weight.shape[1], bytes_accessed=8 * 2**20, transcendentals=0
         ),
         name="project",
     )(weight, part, *([] if before is None else [before]))
@@ -339,6 +333,7 @@
         for start in starts
     ]
     near_lasts = [shifted(last, by_two) for last in lasts]
+    near_first = shifted(first, by_two)
     far = None
     if devices > 8:
         both = jnp.stack((key_proj, value_proj))
@@ -355,9 +350,8 @@
         sources = [own(4, 1, start), own(5, 0, start)]
         sums, marks = attend(meta, query_proj, 1, start, size, sources, None, None, None, "last_own")
         state_last[start] = (sums, marks, 0)
-        first, near_lasts[0], sums = lax.optimization_barrier((first, near_lasts[0], sums))
+        near_lasts[0], sums = lax.optimization_barrier((near_lasts[0], sums))
         state_last[start] = (sums, marks, 0)
-    near_first = shifted(first, by_two)
     near_lasts[0], held = lax.optimization_barrier((near_lasts[0], query_proj))
     sums_first, marks_first = attend(meta, held, 0, 0, heads, [own(0, 0, 0)], None, None, None, "first_own")
     if len(starts) > 1:
@@ -378,6 +372,7 @@
             sources += [own(4, 1, start), own(5, 0, start)]
         outs.append(attend(meta, query_proj, 1, start, size, sources, state, dests, None, "last_rest"))
     weight, *outs = lax.optimization_barrier((weight, *outs))
+    weight = weight.reshape(groups, len(starts), size * LANES // 2, weight.shape[1])
     result = None
     for number, start in enumerate(starts):
         sources = [moved(1, prevs[number], 0, 0), moved(2, near_first, 0, start)]
@@ -386,12 +381,7 @@
         state = (sums_first, marks_first, start)
         out = attend(meta, query_proj, 0, start, size, sources, state, dests, outs[number], "first_rest")
         got = lax.all_to_all(out, "head", split_axis=0, concat_axis=0, tiled=True)
-        layout = tuple(
-            (head // heads, head % heads - start, head)
-            for head in range(groups * heads)
-            if start <= head % heads < start + size
-        )
-        result = project(got, layout, weight, result, start == starts[-1])
+        result = project(got, number, weight, result)
     return result
 
 

time: 418 us -> 388 us (0.928)
  the two profiles are of different devices: /device:TPU:16 before, /device:TPU:24 now
where the time goes in v1:
time: 388 us; the launch traced here: 387 us
  Pallas kernels  337 us (87%)
  starting transfers between devices  16 us (4%)
  between operations  13.7 us (4%)
  waiting for transfers between devices  7.76 us (2%)
  local copies, waits for them, and re-layouts  7.18 us (2%)
  other arithmetic  5.58 us (1%)
    pallas_call x6, Pallas kernels, attend(): pl.pallas_call(functools.partial(attend_kernel, tuple((source[0] for sour...  327 us
    pallas_call x2, Pallas kernels, project(): pl.pallas_call(functools.partial(project_kernel, rows), out_shape=jax.Sha...  9.47 us
    ppermute x5, starting transfers between devices, shifted(): return lax.ppermute(x, 'frame', pairs)  8.11 us
    all_to_all x2, starting transfers between devices, shards(): got = lax.all_to_all(out, 'head', split_axis=0, concat_axis=0, tiled=True)  7.92 us
  transfers between devices with their start and end apart: 8, of which 1 were waited for; matrix products, arithmetic and copies ran while one was open for 2% of the time, Pallas kernels for 86%

profile of v1, /device:TPU:24, one launch (start us, length us, event | category | flops | bytes accessed | tf_op | source)
XLA Modules:
  0.0 386.9 jit_solution(1608585040744295406)
XLA Ops:
  6.5 0.7 all-gather.2.cloned.1.call-update
  7.3 1.5 slice_bitcast_fusion.2
  8.8 0.0 copy-start
  8.8 0.0 copy-start.1
  8.8 1.0 pad_maximum_fusion.1
  9.7 1.4 collective-permute-start
  11.2 1.0 pad_maximum_fusion.2
  12.2 1.3 collective-permute-start.1
  13.5 0.1 slice_bitcast_fusion
  13.6 1.3 pad_maximum_fusion
  14.9 1.3 collective-permute-start.3
  16.2 0.1 stack.59
  16.3 0.2 select_reduce_fusion
  16.5 1.5 copy-done.2
  18.0 51.3 %last_own.1 = (f32[2,80,1536]{2,1,0:T(8,128)S(1)}, f32[2,8,128]{2,1,0:T(8,128)S(1)}) custom-call(s32[8]{0:T(128)S(1)} %broadcast_minimum_fusion.meta_ref, bf16[4,1536,128]{2,1,0:T(8,128)(2,1)S(1)} %copy-done.2, bf16[4,1536,128]{2,1,0:T(8,128)(2,1)S(1)} %copy-done.1, bf16[4,1536,128]{2,1,0:T(8,128)(2,1)S(1)} %copy-done.1, bf16[4,1536,128]{2,1,0:T(8,128)(2,1)S(1)} %copy-done, ...), custom_call_target="tpu_custom_call" | custom-call | flops 9663676416 | bytes 3145728 | tf_op jit(solution)/shard_map/last_own/pallas_call | solution.py:233
  69.3 1.0 broadcast_select_fusion
  70.3 2.0 collective-permute-start.4
  72.4 61.9 %first_own.1 = (f32[4,80,1536]{2,1,0:T(8,128)S(1)}, f32[4,8,128]{2,1,0:T(8,128)S(1)}) custom-call(s32[8]{0:T(128)S(1)} %broadcast_minimum_fusion.meta_ref, bf16[4,1536,128]{2,1,0:T(8,128)(2,1)S(1)} %copy-done.2, bf16[4,1536,128]{2,1,0:T(8,128)(2,1)S(1)} %copy-done.1, bf16[4,1536,128]{2,1,0:T(8,128)(2,1)S(1)} %copy-done), custom_call_target="tpu_custom_call" | custom-call | flops 9663676416 | bytes 6291456 | tf_op jit(solution)/shard_map/first_own/pallas_call | solution.py:233
  134.3 1.1 broadcast_select_fusion.1
  135.5 2.1 collective-permute-start.2
  137.6 68.3 %last_rest.3.refs_6_ = bf16[4,2,384,128]{3,2,1,0:T(8,128)(2,1)} custom-call(s32[8]{0:T(128)S(1)} %broadcast_minimum_fusion.meta_ref, bf16[4,1536,128]{2,1,0:T(8,128)(2,1)S(1)} %copy-done.2, bf16[2,2,768,128]{3,2,1,0:T(8,128)(2,1)} %collective-permute-done.1.refs_0_.refs_3_, bf16[4,1536,128]{2,1,0:T(8,128)(2,1)S(1)} %copy-done.1, ...), custom_call_target="tpu_custom_call" | custom-call | flops 3623878656 | bytes 3145728 | tf_op jit(solution)/shard_map/last_rest/pallas_call | solution.py:233
  205.9 18.4 %last_rest.2.refs_6_ = bf16[4,2,384,128]{3,2,1,0:T(8,128)(2,1)} custom-call(s32[8]{0:T(128)S(1)} %broadcast_minimum_fusion.meta_ref, bf16[4,1536,128]{2,1,0:T(8,128)(2,1)S(1)} %copy-done.2, bf16[2,2,768,128]{3,2,1,0:T(8,128)(2,1)} %collective-permute-done.refs_0_.refs_1_, bf16[2,2,768,128]{3,2,1,0:T(8,128)(2,1)} %collective-permute-done.refs_0_.refs_1_, ...), custom_call_target="tpu_custom_call" | custom-call | flops 1207959552 | bytes 3145728 | tf_op jit(solution)/shard_map/last_rest/pallas_call | solution.py:233
  224.3 1.5 copy-done.5
  225.8 63.7 %first_rest.3 = bf16[4,2,384,128]{3,2,1,0:T(8,128)(2,1)} custom-call(s32[8]{0:T(128)S(1)} %broadcast_minimum_fusion.meta_ref, bf16[4,1536,128]{2,1,0:T(8,128)(2,1)S(1)} %copy-done.3, bf16[2,2,768,128]{3,2,1,0:T(8,128)(2,1)} %collective-permute-done.4.refs_0_.refs_2_, ...), custom_call_target="tpu_custom_call", output_to_operand_aliasing={{}: (8, {})} | custom-call | flops 2415919104 | bytes 3145728 | tf_op jit(solution)/shard_map/first_rest/pallas_call | solution.py:233
  289.5 4.4 %all-to-all-start.1 = ((bf16[4,2,384,128]{3,2,1,0:T(8,128)(2,1)}), bf16[4,2,384,128]{3,2,1,0:T(8,128)(2,1)}, u32[]{:S(2)}, u32[]{:S(2)}) async-start(bf16[4,2,384,128]{3,2,1,0:T(8,128)(2,1)} %first_rest.3), calls=%async_computation.1 | async-start | bytes 1572864 | tf_op jit(solution)/shard_map/all_to_all | solution.py:383
  293.9 1.5 copy-done.6
  295.5 63.7 %first_rest.2 = bf16[4,2,384,128]{3,2,1,0:T(8,128)(2,1)} custom-call(s32[8]{0:T(128)S(1)} %broadcast_minimum_fusion.meta_ref, bf16[4,1536,128]{2,1,0:T(8,128)(2,1)S(1)} %copy-done.3, bf16[2,2,768,128]{3,2,1,0:T(8,128)(2,1)} %collective-permute-done.2.refs_0_.refs_2_, ...), custom_call_target="tpu_custom_call", output_to_operand_aliasing={{}: (8, {})} | custom-call | flops 2415919104 | bytes 3145728 | tf_op jit(solution)/shard_map/first_rest/pallas_call | solution.py:233
  359.2 3.5 all-to-all-start
  362.7 4.6 %project.2.refs_0_ = bf16[768,1024]{1,0:T(8,128)(2,1)} custom-call(bf16[4,2,128,1024]{3,2,1,0:T(8,128)(2,1)} %bitcast.20, bf16[4,2,384,128]{3,2,1,0:T(8,128)(2,1)} %all-to-all-done.1.part_ref), custom_call_target="tpu_custom_call" | custom-call | flops 805306368 | bytes 8388608 | tf_op jit(solution)/shard_map/project/pallas_call | solution.py:291
  367.3 7.0 %all-to-all-done.part_ref = bf16[4,2,384,128]{3,2,1,0:T(8,128)(2,1)S(1)} async-done(((bf16[4,2,384,128]{3,2,1,0:T(8,128)(2,1)}), bf16[4,2,384,128]{3,2,1,0:T(8,128)(2,1)S(1)}, u32[]{:S(2)}, u32[]{:S(2)}) %all-to-all-start) | async-done | bytes 786464 | tf_op jit(solution)/shard_map/all_to_all | solution.py:383
  374.3 0.9 copy-done.13
  375.2 4.9 %project.3 = bf16[768,1024]{1,0:T(8,128)(2,1)} custom-call(bf16[4,2,128,1024]{3,2,1,0:T(8,128)(2,1)} %bitcast.21, bf16[4,2,384,128]{3,2,1,0:T(8,128)(2,1)} %copy-done.13, bf16[768,1024]{1,0:T(8,128)(2,1)} %project.2.refs_0_), custom_call_target="tpu_custom_call" | custom-call | flops 805306368 | bytes 8388608 | tf_op jit(solution)/shard_map/project/pallas_call | solution.py:291
  (33 shorter events, 0.1 us)
Async XLA Ops:
  6.5 217.7 %all-gather.2.cloned.1.call-start = ((), (), s32[]{:S(2)}) async-start(), calls=%async_computation.2 | async-start | bytes 2621440 | tf_op jit(solution)/shard_map/all_gather | solution.py:320
  8.7 3.4 copy-start.7
  8.7 3.4 copy-start.9
  8.7 3.4 copy-start.11
  8.8 4.7 %copy-start = (bf16[4,1536,128]{2,1,0:T(8,128)(2,1)S(1)}, bf16[4,1536,128]{2,1,0:T(8,128)(2,1)}, u32[]{:S(2)}) copy-start(bf16[4,1536,128]{2,1,0:T(8,128)(2,1)} %refs_5_.1) | copy-start | bytes 4718596
  8.8 4.7 %copy-start.1 = (bf16[4,1536,128]{2,1,0:T(8,128)(2,1)S(1)}, bf16[4,1536,128]{2,1,0:T(8,128)(2,1)}, u32[]{:S(2)}) copy-start(bf16[4,1536,128]{2,1,0:T(8,128)(2,1)} %refs_2_.3) | copy-start | bytes 4718596
  9.7 59.6 %collective-permute-start = (bf16[2,2,768,128]{3,2,1,0:T(8,128)(2,1)}, bf16[2,2,768,128]{3,2,1,0:T(8,128)(2,1)}, u32[]{:S(2)}, u32[]{:S(2)}) collective-permute-start(bf16[2,2,768,128]{3,2,1,0:T(8,128)(2,1)} %pad_maximum_fusion.1), channel_id=1, source_target_pairs={{0,8},{4,12},{8,16},{12,20},{16,24},{20,28},{1,9},{5,13},{9,17},{1... | collective-permute-start | bytes 2359304 | tf_op jit(solution)/shard_map/ppermute | solution.py:310
  12.2 122.2 %collective-permute-start.1 = (bf16[2,2,768,128]{3,2,1,0:T(8,128)(2,1)}, bf16[2,2,768,128]{3,2,1,0:T(8,128)(2,1)}, u32[]{:S(2)}, u32[]{:S(2)}) collective-permute-start(bf16[2,2,768,128]{3,2,1,0:T(8,128)(2,1)} %pad_maximum_fusion.2), channel_id=1, source_target_pairs={{0,8},{4,12},{8,16},{12,20},{16,24},{20,28},{1,9},{5,13},{9,17},{1... | collective-permute-start | bytes 2359304 | tf_op jit(solution)/shard_map/ppermute | solution.py:310
  13.6 2.7 copy-start.14
  14.9 209.4 %collective-permute-start.3 = (bf16[2,4,768,128]{3,2,1,0:T(8,128)(2,1)}, bf16[2,4,768,128]{3,2,1,0:T(8,128)(2,1)}, u32[]{:S(2)}, u32[]{:S(2)}) collective-permute-start(bf16[2,4,768,128]{3,2,1,0:T(8,128)(2,1)} %pad_maximum_fusion), channel_id=1, source_target_pairs={{0,8},{4,12},{8,16},{12,20},{16,24},{20,28},{1,9},{5,13},{9,17},{1... | collective-permute-start | bytes 4718600 | tf_op jit(solution)/shard_map/ppermute | solution.py:310
  16.5 1.5 copy-start.2
  18.0 51.3 %copy-start.12 = (bf16[1,2,768,128]{3,2,1,0:T(8,128)(2,1)S(1)}, bf16[1,2,768,128]{3,2,1,0:T(8,128)(2,1)}, u32[]{:S(2)}) copy-start(bf16[1,2,768,128]{3,2,1,0:T(8,128)(2,1)} %copy-done.11) | copy-start | bytes 1179652
  70.3 64.0 %copy-start.8 = (bf16[1,2,768,128]{3,2,1,0:T(8,128)(2,1)S(1)}, bf16[1,2,768,128]{3,2,1,0:T(8,128)(2,1)}, u32[]{:S(2)}) copy-start(bf16[1,2,768,128]{3,2,1,0:T(8,128)(2,1)} %copy-done.7) | copy-start | bytes 1179652
  70.3 64.0 %copy-start.10 = (bf16[1,2,768,128]{3,2,1,0:T(8,128)(2,1)S(1)}, bf16[1,2,768,128]{3,2,1,0:T(8,128)(2,1)}, u32[]{:S(2)}) copy-start(bf16[1,2,768,128]{3,2,1,0:T(8,128)(2,1)} %copy-done.9) | copy-start | bytes 1179652
  70.3 153.9 %collective-permute-start.4 = (bf16[2,2,768,128]{3,2,1,0:T(8,128)(2,1)}, bf16[2,2,768,128]{3,2,1,0:T(8,128)(2,1)}, u32[]{:S(2)}, u32[]{:S(2)}) collective-permute-start(bf16[2,2,768,128]{3,2,1,0:T(8,128)(2,1)} %broadcast_select_fusion), channel_id=1, source_target_pairs={{12,8},{20,16},{28,24},{0,4},{8,12},{16,20},{24,28},{13,9},{21,17}... | collective-permute-start | bytes 2359304 | tf_op jit(solution)/shard_map/ppermute | solution.py:310
  134.3 71.6 %copy-start.4 = (f32[4,80,1536]{2,1,0:T(8,128)}, f32[4,80,1536]{2,1,0:T(8,128)S(1)}, u32[]{:S(2)}) copy-start(f32[4,80,1536]{2,1,0:T(8,128)S(1)} %get-tuple-element.27.refs_4_) | copy-start | bytes 5898244
  135.5 158.5 %collective-permute-start.2 = (bf16[2,2,768,128]{3,2,1,0:T(8,128)(2,1)}, bf16[2,2,768,128]{3,2,1,0:T(8,128)(2,1)}, u32[]{:S(2)}, u32[]{:S(2)}) collective-permute-start(bf16[2,2,768,128]{3,2,1,0:T(8,128)(2,1)} %broadcast_select_fusion.1), channel_id=1, source_target_pairs={{12,8},{20,16},{28,24},{0,4},{8,12},{16,20},{24,28},{13,9},{21,17}... | collective-permute-start | bytes 2359304 | tf_op jit(solution)/shard_map/ppermute | solution.py:310
  205.9 18.4 %copy-start.3 = (bf16[4,1536,128]{2,1,0:T(8,128)(2,1)S(1)}, bf16[4,1536,128]{2,1,0:T(8,128)(2,1)}, u32[]{:S(2)}) copy-start(bf16[4,1536,128]{2,1,0:T(8,128)(2,1)} %q_ref.10) | copy-start | bytes 4718596
  224.3 1.5 copy-start.5
  289.5 69.7 %all-to-all-start.1 = ((bf16[4,2,384,128]{3,2,1,0:T(8,128)(2,1)}), bf16[4,2,384,128]{3,2,1,0:T(8,128)(2,1)}, u32[]{:S(2)}, u32[]{:S(2)}) async-start(bf16[4,2,384,128]{3,2,1,0:T(8,128)(2,1)} %first_rest.3), calls=%async_computation.1 | async-start | bytes 1572864 | tf_op jit(solution)/shard_map/all_to_all | solution.py:383
  293.9 1.5 copy-start.6
  359.2 15.1 %all-to-all-start = ((bf16[4,2,384,128]{3,2,1,0:T(8,128)(2,1)}), bf16[4,2,384,128]{3,2,1,0:T(8,128)(2,1)S(1)}, u32[]{:S(2)}, u32[]{:S(2)}) async-start(bf16[4,2,384,128]{3,2,1,0:T(8,128)(2,1)} %first_rest.2), calls=%async_computation | async-start | bytes 1572864 | tf_op jit(solution)/shard_map/all_to_all | solution.py:383
  374.3 0.9 copy-start.13
Sparse Core Ops, SparseCore 0:
  8.9 23.5 all-gather.1

commit v2 on v1

--- a/solution.py
+++ b/solution.py
@@ -133,13 +133,12 @@
 
         lax.fori_loop(0, total // 4, whole, 0)
 
-        @pl.when(total % 4 >= 2)
-        def _():
-            tiles([(total // 4 * 4, 2)])
-
-        @pl.when(total % 2 == 1)
-        def _():
-            tiles([(total - 1, 1)])
+        first = total // 4 * 4
+        for rest in (1, 2, 3):
+
+            @pl.when(total % 4 == rest)
+            def _(rest=rest):
+                tiles([(first, 2)] * (rest > 1) + [(total - 1, 1)] * (rest % 2))
 
     @pl.when(jnp.logical_not(safe))
     def _():
@@ -327,13 +326,9 @@
     size = heads // 2 if heads % 2 == 0 else heads
     starts = range(0, heads, size)
     by_two = [(i, i + 2) for i in range(devices - 2)]
-    first = jnp.stack((key_proj[:, :half], value_proj[:, :half]))
-    lasts = [
-        jnp.stack((key_proj[start : start + size, half:], value_proj[start : start + size, half:]))
-        for start in starts
-    ]
+    cuts = [slice(start, start + size) for start in starts]
+    lasts = [jnp.stack((key_proj[cut, half:], value_proj[cut, half:])) for cut in cuts]
     near_lasts = [shifted(last, by_two) for last in lasts]
-    near_first = shifted(first, by_two)
     far = None
     if devices > 8:
         both = jnp.stack((key_proj, value_proj))
@@ -346,16 +341,21 @@
         return slot, (array, 0, part, start), (array, 1, part, start)
 
     state_last = {}
+    held_keys, held_values = key_proj, value_proj
     for start in starts[:-1]:
         sources = [own(4, 1, start), own(5, 0, start)]
         sums, marks = attend(meta, query_proj, 1, start, size, sources, None, None, None, "last_own")
         state_last[start] = (sums, marks, 0)
+        held_keys, held_values, sums = lax.optimization_barrier((held_keys, held_values, sums))
         near_lasts[0], sums = lax.optimization_barrier((near_lasts[0], sums))
         state_last[start] = (sums, marks, 0)
+    firsts = [jnp.stack((held_keys[cut, :half], held_values[cut, :half])) for cut in cuts]
+    near_lasts[0], firsts[0] = lax.optimization_barrier((near_lasts[0], firsts[0]))
     near_lasts[0], held = lax.optimization_barrier((near_lasts[0], query_proj))
     sums_first, marks_first = attend(meta, held, 0, 0, heads, [own(0, 0, 0)], None, None, None, "first_own")
     if len(starts) > 1:
-        near_lasts[1], sums_first = lax.optimization_barrier((near_lasts[1], sums_first))
+        near_lasts[1], sums_first, *firsts[1:] = lax.optimization_barrier((near_lasts[1], sums_first, *firsts[1:]))
+    near_firsts = [shifted(first, by_two) for first in firsts]
     to_even = [(i + 1, i) for i in range(2, devices - 1, 2)]
     to_odd = [(i, i + 1) for i in range(0, devices - 1, 2)]
     prevs = [
@@ -375,7 +375,7 @@
     weight = weight.reshape(groups, len(starts), size * LANES // 2, weight.shape[1])
     result = None
     for number, start in enumerate(starts):
-        sources = [moved(1, prevs[number], 0, 0), moved(2, near_first, 0, start)]
+        sources = [moved(1, prevs[number], 0, 0), moved(2, near_firsts[number], 0, 0)]
         if far is not None:
             sources.append(moved(3, far, 0, start))
         state = (sums_first, marks_first, start)

time: 388 us -> 377 us (0.972)
  the two profiles are of different devices: /device:TPU:24 before, /device:TPU:16 now
where the time goes in v2:
time: 377 us; the launch traced here: 372 us
  Pallas kernels  297 us (79%)
  starting transfers between devices  38 us (10%)
  between operations  13.7 us (4%)
  local copies, waits for them, and re-layouts  9.4 us (2%)
  waiting for transfers between devices  7.76 us (2%)
  other arithmetic  6.09 us (2%)
    pallas_call x6, Pallas kernels, attend(): pl.pallas_call(functools.partial(attend_kernel, tuple((source[0] for sour...  287 us
    ppermute x6, starting transfers between devices, shifted(): return lax.ppermute(x, 'frame', pairs)  30.4 us
    pallas_call x2, Pallas kernels, project(): pl.pallas_call(functools.partial(project_kernel, rows), out_shape=jax.Sha...  9.47 us
    unnamed x36, local copies, waits for them, and re-layouts  7.74 us
    all_to_all x2, starting transfers between devices, shards(): got = lax.all_to_all(out, 'head', split_axis=0, concat_axis=0, tiled=True)  7.67 us
  transfers between devices with their start and end apart: 9, of which 1 were waited for; matrix products, arithmetic and copies ran while one was open for 2% of the time, Pallas kernels for 79%

profile of v2, /device:TPU:16, one launch (start us, length us, event | category | flops | bytes accessed | tf_op | source)
XLA Modules:
  0.0 371.9 jit_solution(9227247432051313398)
XLA Ops:
  6.5 0.7 all-gather.2.cloned.1.call-update
  7.3 1.5 slice_bitcast_fusion.2
  8.8 1.0 pad_maximum_fusion
  9.8 3.6 collective-permute-start
  13.4 1.0 pad_maximum_fusion.2
  14.3 1.9 collective-permute-start.1
  16.4 0.2 select_reduce_fusion
  16.6 1.5 copy-done.2
  18.1 56.3 %last_own.1 = (f32[2,80,1536]{2,1,0:T(8,128)S(1)}, f32[2,8,128]{2,1,0:T(8,128)S(1)}) custom-call(s32[8]{0:T(128)S(1)} %broadcast_minimum_fusion.meta_ref, bf16[4,1536,128]{2,1,0:T(8,128)(2,1)S(1)} %copy-done.2, bf16[4,1536,128]{2,1,0:T(8,128)(2,1)S(1)} %copy-done.1, bf16[4,1536,128]{2,1,0:T(8,128)(2,1)S(1)} %copy-done.1, bf16[4,1536,128]{2,1,0:T(8,128)(2,1)S(1)} %copy-done, ...), custom_call_target="tpu_custom_call" | custom-call | flops 9663676416 | bytes 3145728 | tf_op jit(solution)/shard_map/last_own/pallas_call | solution.py:232
  74.4 0.9 copy-done.5
  75.4 0.9 pad_maximum_fusion.3
  76.4 1.0 pad_maximum_fusion.1
  77.4 1.0 broadcast_select_fusion
  78.4 2.0 collective-permute-start.4
  80.5 5.5 %collective-permute-start.5 = (bf16[2,2,768,128]{3,2,1,0:T(8,128)(2,1)}, bf16[2,2,768,128]{3,2,1,0:T(8,128)(2,1)}, u32[]{:S(2)}, u32[]{:S(2)}) collective-permute-start(bf16[2,2,768,128]{3,2,1,0:T(8,128)(2,1)} %pad_maximum_fusion.1), channel_id=1, source_target_pairs={{0,8},{4,12},{8,16},{12,20},{16,24},{20,28},{1,9},{5,13},{9,17},{1... | collective-permute-start | bytes 2359304 | tf_op jit(solution)/shard_map/ppermute | solution.py:309
  86.0 52.0 %first_own.1 = (f32[4,80,1536]{2,1,0:T(8,128)S(1)}, f32[4,8,128]{2,1,0:T(8,128)S(1)}) custom-call(s32[8]{0:T(128)S(1)} %broadcast_minimum_fusion.meta_ref, bf16[4,1536,128]{2,1,0:T(8,128)(2,1)S(1)} %copy-done.3, bf16[4,1536,128]{2,1,0:T(8,128)(2,1)S(1)} %copy-done.1, bf16[4,1536,128]{2,1,0:T(8,128)(2,1)S(1)} %copy-done), custom_call_target="tpu_custom_call" | custom-call | flops 9663676416 | bytes 6291456 | tf_op jit(solution)/shard_map/first_own/pallas_call | solution.py:232
  138.0 1.3 copy-done.7
  139.3 11.3 %collective-permute-start.3 = (bf16[2,2,768,128]{3,2,1,0:T(8,128)(2,1)}, bf16[2,2,768,128]{3,2,1,0:T(8,128)(2,1)}, u32[]{:S(2)}, u32[]{:S(2)}) collective-permute-start(bf16[2,2,768,128]{3,2,1,0:T(8,128)(2,1)} %pad_maximum_fusion.3), channel_id=1, source_target_pairs={{0,8},{4,12},{8,16},{12,20},{16,24},{20,28},{1,9},{5,13},{9,17},{1... | collective-permute-start | bytes 2359304 | tf_op jit(solution)/shard_map/ppermute | solution.py:309
  150.6 1.0 broadcast_select_fusion.1
  151.6 6.0 %collective-permute-start.2 = (bf16[2,2,768,128]{3,2,1,0:T(8,128)(2,1)}, bf16[2,2,768,128]{3,2,1,0:T(8,128)(2,1)}, u32[]{:S(2)}, u32[]{:S(2)}) collective-permute-start(bf16[2,2,768,128]{3,2,1,0:T(8,128)(2,1)} %broadcast_select_fusion.1), channel_id=1, source_target_pairs={{12,8},{20,16},{28,24},{0,4},{8,12},{16,20},{24,28},{13,9},{21,17}... | collective-permute-start | bytes 2359304 | tf_op jit(solution)/shard_map/ppermute | solution.py:309
  157.6 68.3 %last_rest.3.refs_6_ = bf16[4,2,384,128]{3,2,1,0:T(8,128)(2,1)} custom-call(s32[8]{0:T(128)S(1)} %broadcast_minimum_fusion.meta_ref, bf16[4,1536,128]{2,1,0:T(8,128)(2,1)S(1)} %copy-done.3, bf16[2,2,768,128]{3,2,1,0:T(8,128)(2,1)} %collective-permute-done.1.refs_0_.refs_3_, bf16[4,1536,128]{2,1,0:T(8,128)(2,1)S(1)} %copy-done.1, ...), custom_call_target="tpu_custom_call" | custom-call | flops 3623878656 | bytes 3145728 | tf_op jit(solution)/shard_map/last_rest/pallas_call | solution.py:232
  225.9 13.3 %last_rest.2.refs_6_ = bf16[4,2,384,128]{3,2,1,0:T(8,128)(2,1)} custom-call(s32[8]{0:T(128)S(1)} %broadcast_minimum_fusion.meta_ref, bf16[4,1536,128]{2,1,0:T(8,128)(2,1)S(1)} %copy-done.3, bf16[2,2,768,128]{3,2,1,0:T(8,128)(2,1)} %collective-permute-done.refs_0_.refs_1_, bf16[2,2,768,128]{3,2,1,0:T(8,128)(2,1)} %collective-permute-done.refs_0_.refs_1_, ...), custom_call_target="tpu_custom_call" | custom-call | flops 1207959552 | bytes 3145728 | tf_op jit(solution)/shard_map/last_rest/pallas_call | solution.py:232
  239.3 1.5 copy-done.8
  240.8 48.9 %first_rest.3 = bf16[4,2,384,128]{3,2,1,0:T(8,128)(2,1)} custom-call(s32[8]{0:T(128)S(1)} %broadcast_minimum_fusion.meta_ref, bf16[4,1536,128]{2,1,0:T(8,128)(2,1)S(1)} %copy-done.4, bf16[2,2,768,128]{3,2,1,0:T(8,128)(2,1)} %collective-permute-done.4.refs_0_.refs_2_, ...), custom_call_target="tpu_custom_call", output_to_operand_aliasing={{}: (8, {})} | custom-call | flops 2415919104 | bytes 3145728 | tf_op jit(solution)/shard_map/first_rest/pallas_call | solution.py:232
  289.7 4.2 %all-to-all-start.1 = ((bf16[4,2,384,128]{3,2,1,0:T(8,128)(2,1)}), bf16[4,2,384,128]{3,2,1,0:T(8,128)(2,1)}, u32[]{:S(2)}, u32[]{:S(2)}) async-start(bf16[4,2,384,128]{3,2,1,0:T(8,128)(2,1)} %first_rest.3), calls=%async_computation.1 | async-start | bytes 1572864 | tf_op jit(solution)/shard_map/all_to_all | solution.py:383
  293.9 1.5 copy-done.9
  295.4 48.7 %first_rest.2 = bf16[4,2,384,128]{3,2,1,0:T(8,128)(2,1)} custom-call(s32[8]{0:T(128)S(1)} %broadcast_minimum_fusion.meta_ref, bf16[4,1536,128]{2,1,0:T(8,128)(2,1)S(1)} %copy-done.4, bf16[2,2,768,128]{3,2,1,0:T(8,128)(2,1)} %collective-permute-done.2.refs_0_.refs_2_, ...), custom_call_target="tpu_custom_call", output_to_operand_aliasing={{}: (8, {})} | custom-call | flops 2415919104 | bytes 3145728 | tf_op jit(solution)/shard_map/first_rest/pallas_call | solution.py:232
  344.1 3.5 all-to-all-start
  347.6 4.6 %project.2.refs_0_ = bf16[768,1024]{1,0:T(8,128)(2,1)} custom-call(bf16[4,2,128,1024]{3,2,1,0:T(8,128)(2,1)} %bitcast.24, bf16[4,2,384,128]{3,2,1,0:T(8,128)(2,1)} %all-to-all-done.1.part_ref), custom_call_target="tpu_custom_call" | custom-call | flops 805306368 | bytes 8388608 | tf_op jit(solution)/shard_map/project/pallas_call | solution.py:290
  352.2 7.0 %all-to-all-done.part_ref = bf16[4,2,384,128]{3,2,1,0:T(8,128)(2,1)S(1)} async-done(((bf16[4,2,384,128]{3,2,1,0:T(8,128)(2,1)}), bf16[4,2,384,128]{3,2,1,0:T(8,128)(2,1)S(1)}, u32[]{:S(2)}, u32[]{:S(2)}) %all-to-all-start) | async-done | bytes 786464 | tf_op jit(solution)/shard_map/all_to_all | solution.py:383
  359.2 0.9 copy-done.16
  360.1 4.9 %project.3 = bf16[768,1024]{1,0:T(8,128)(2,1)} custom-call(bf16[4,2,128,1024]{3,2,1,0:T(8,128)(2,1)} %bitcast.25, bf16[4,2,384,128]{3,2,1,0:T(8,128)(2,1)} %copy-done.16, bf16[768,1024]{1,0:T(8,128)(2,1)} %project.2.refs_0_), custom_call_target="tpu_custom_call" | custom-call | flops 805306368 | bytes 8388608 | tf_op jit(solution)/shard_map/project/pallas_call | solution.py:290
  (42 shorter events, 0.3 us)
Async XLA Ops:
  6.5 232.7 %all-gather.2.cloned.1.call-start = ((), (), s32[]{:S(2)}) async-start(), calls=%async_computation.2 | async-start | bytes 2621440 | tf_op jit(solution)/shard_map/all_gather | solution.py:319
  8.7 5.6 %copy-start.10 = (bf16[1,2,768,128]{3,2,1,0:T(8,128)(2,1)}, bf16[1,2,768,128]{3,2,1,0:T(8,128)(2,1)S(1)}, u32[]{:S(2)}) copy-start(bf16[1,2,768,128]{3,2,1,0:T(8,128)(2,1)S(1)} %get-tuple-element.49) | copy-start | bytes 1179652
  8.7 5.6 %copy-start.12 = (bf16[1,2,768,128]{3,2,1,0:T(8,128)(2,1)}, bf16[1,2,768,128]{3,2,1,0:T(8,128)(2,1)S(1)}, u32[]{:S(2)}) copy-start(bf16[1,2,768,128]{3,2,1,0:T(8,128)(2,1)S(1)} %get-tuple-element.52) | copy-start | bytes 1179652
  8.8 5.6 %copy-start.14 = (bf16[1,2,768,128]{3,2,1,0:T(8,128)(2,1)}, bf16[1,2,768,128]{3,2,1,0:T(8,128)(2,1)S(1)}, u32[]{:S(2)}) copy-start(bf16[1,2,768,128]{3,2,1,0:T(8,128)(2,1)S(1)} %get-tuple-element.51) | copy-start | bytes 1179652
  8.8 7.6 %copy-start.17 = (s32[16]{0:T(128)S(1)}, s32[16]{0:T(128)}, u32[]{:S(2)}) copy-start(s32[16]{0:T(128)} %param.8) | copy-start | bytes 196
  8.8 7.8 %copy-start = (bf16[4,1536,128]{2,1,0:T(8,128)(2,1)S(1)}, bf16[4,1536,128]{2,1,0:T(8,128)(2,1)}, u32[]{:S(2)}) copy-start(bf16[4,1536,128]{2,1,0:T(8,128)(2,1)} %refs_5_.1) | copy-start | bytes 4718596
  8.8 7.8 %copy-start.1 = (bf16[4,1536,128]{2,1,0:T(8,128)(2,1)S(1)}, bf16[4,1536,128]{2,1,0:T(8,128)(2,1)}, u32[]{:S(2)}) copy-start(bf16[4,1536,128]{2,1,0:T(8,128)(2,1)} %refs_2_.3) | copy-start | bytes 4718596
  9.8 67.6 %collective-permute-start = (bf16[2,2,768,128]{3,2,1,0:T(8,128)(2,1)}, bf16[2,2,768,128]{3,2,1,0:T(8,128)(2,1)}, u32[]{:S(2)}, u32[]{:S(2)}) collective-permute-start(bf16[2,2,768,128]{3,2,1,0:T(8,128)(2,1)} %pad_maximum_fusion), channel_id=1, source_target_pairs={{0,8},{4,12},{8,16},{12,20},{16,24},{20,28},{1,9},{5,13},{9,17},{1... | collective-permute-start | bytes 2359304 | tf_op jit(solution)/shard_map/ppermute | solution.py:309
  14.3 124.9 %collective-permute-start.1 = (bf16[2,2,768,128]{3,2,1,0:T(8,128)(2,1)}, bf16[2,2,768,128]{3,2,1,0:T(8,128)(2,1)}, u32[]{:S(2)}, u32[]{:S(2)}) collective-permute-start(bf16[2,2,768,128]{3,2,1,0:T(8,128)(2,1)} %pad_maximum_fusion.2), channel_id=1, source_target_pairs={{0,8},{4,12},{8,16},{12,20},{16,24},{20,28},{1,9},{5,13},{9,17},{1... | collective-permute-start | bytes 2359304 | tf_op jit(solution)/shard_map/ppermute | solution.py:309
  16.6 1.5 copy-start.2
  74.4 0.9 copy-start.5
  75.4 2.0 copy-start.15
  77.4 8.6 %copy-start.3 = (bf16[4,1536,128]{2,1,0:T(8,128)(2,1)S(1)}, bf16[4,1536,128]{2,1,0:T(8,128)(2,1)}, u32[]{:S(2)}) copy-start(bf16[4,1536,128]{2,1,0:T(8,128)(2,1)} %q_ref.10) | copy-start | bytes 4718596
  78.4 72.2 %copy-start.11 = (bf16[1,2,768,128]{3,2,1,0:T(8,128)(2,1)S(1)}, bf16[1,2,768,128]{3,2,1,0:T(8,128)(2,1)}, u32[]{:S(2)}) copy-start(bf16[1,2,768,128]{3,2,1,0:T(8,128)(2,1)} %copy-done.10) | copy-start | bytes 1179652
  78.4 72.2 %copy-start.13 = (bf16[1,2,768,128]{3,2,1,0:T(8,128)(2,1)S(1)}, bf16[1,2,768,128]{3,2,1,0:T(8,128)(2,1)}, u32[]{:S(2)}) copy-start(bf16[1,2,768,128]{3,2,1,0:T(8,128)(2,1)} %copy-done.12) | copy-start | bytes 1179652
  78.4 160.8 %collective-permute-start.4 = (bf16[2,2,768,128]{3,2,1,0:T(8,128)(2,1)}, bf16[2,2,768,128]{3,2,1,0:T(8,128)(2,1)}, u32[]{:S(2)}, u32[]{:S(2)}) collective-permute-start(bf16[2,2,768,128]{3,2,1,0:T(8,128)(2,1)} %broadcast_select_fusion), channel_id=1, source_target_pairs={{12,8},{20,16},{28,24},{0,4},{8,12},{16,20},{24,28},{13,9},{21,17}... | collective-permute-start | bytes 2359304 | tf_op jit(solution)/shard_map/ppermute | solution.py:309
  80.5 158.8 %collective-permute-start.5 = (bf16[2,2,768,128]{3,2,1,0:T(8,128)(2,1)}, bf16[2,2,768,128]{3,2,1,0:T(8,128)(2,1)}, u32[]{:S(2)}, u32[]{:S(2)}) collective-permute-start(bf16[2,2,768,128]{3,2,1,0:T(8,128)(2,1)} %pad_maximum_fusion.1), channel_id=1, source_target_pairs={{0,8},{4,12},{8,16},{12,20},{16,24},{20,28},{1,9},{5,13},{9,17},{1... | collective-permute-start | bytes 2359304 | tf_op jit(solution)/shard_map/ppermute | solution.py:309
  138.0 1.3 copy-start.7
  139.3 154.6 %collective-permute-start.3 = (bf16[2,2,768,128]{3,2,1,0:T(8,128)(2,1)}, bf16[2,2,768,128]{3,2,1,0:T(8,128)(2,1)}, u32[]{:S(2)}, u32[]{:S(2)}) collective-permute-start(bf16[2,2,768,128]{3,2,1,0:T(8,128)(2,1)} %pad_maximum_fusion.3), channel_id=1, source_target_pairs={{0,8},{4,12},{8,16},{12,20},{16,24},{20,28},{1,9},{5,13},{9,17},{1... | collective-permute-start | bytes 2359304 | tf_op jit(solution)/shard_map/ppermute | solution.py:309
  151.6 74.3 %copy-start.6 = (f32[2,80,1536]{2,1,0:T(8,128)S(1)}, f32[2,80,1536]{2,1,0:T(8,128)}, u32[]{:S(2)}) copy-start(f32[2,80,1536]{2,1,0:T(8,128)} %copy-done.5) | copy-start | bytes 2949124
  151.6 142.3 %collective-permute-start.2 = (bf16[2,2,768,128]{3,2,1,0:T(8,128)(2,1)}, bf16[2,2,768,128]{3,2,1,0:T(8,128)(2,1)}, u32[]{:S(2)}, u32[]{:S(2)}) collective-permute-start(bf16[2,2,768,128]{3,2,1,0:T(8,128)(2,1)} %broadcast_select_fusion.1), channel_id=1, source_target_pairs={{12,8},{20,16},{28,24},{0,4},{8,12},{16,20},{24,28},{13,9},{21,17}... | collective-permute-start | bytes 2359304 | tf_op jit(solution)/shard_map/ppermute | solution.py:309
  225.9 13.4 %copy-start.4 = (bf16[4,1536,128]{2,1,0:T(8,128)(2,1)S(1)}, bf16[4,1536,128]{2,1,0:T(8,128)(2,1)}, u32[]{:S(2)}) copy-start(bf16[4,1536,128]{2,1,0:T(8,128)(2,1)} %q_ref.10) | copy-start | bytes 4718596
  239.3 1.5 copy-start.8
  289.7 54.4 %all-to-all-start.1 = ((bf16[4,2,384,128]{3,2,1,0:T(8,128)(2,1)}), bf16[4,2,384,128]{3,2,1,0:T(8,128)(2,1)}, u32[]{:S(2)}, u32[]{:S(2)}) async-start(bf16[4,2,384,128]{3,2,1,0:T(8,128)(2,1)} %first_rest.3), calls=%async_computation.1 | async-start | bytes 1572864 | tf_op jit(solution)/shard_map/all_to_all | solution.py:383
  293.9 1.5 copy-start.9
  344.1 15.1 %all-to-all-start = ((bf16[4,2,384,128]{3,2,1,0:T(8,128)(2,1)}), bf16[4,2,384,128]{3,2,1,0:T(8,128)(2,1)S(1)}, u32[]{:S(2)}, u32[]{:S(2)}) async-start(bf16[4,2,384,128]{3,2,1,0:T(8,128)(2,1)} %first_rest.2), calls=%async_computation | async-start | bytes 1572864 | tf_op jit(solution)/shard_map/all_to_all | solution.py:383
  359.2 0.9 copy-start.16
Sparse Core Ops, SparseCore 0:
  8.9 23.6 all-gather.1
